TPU v7x, 32 devices: a whole 2x2x4 slice. The times are simulated.
32 devices in a mesh: head: 4 (over z), ctx: 8 (over y, x, core).
Axes of the slice: x: 2, y: 2, z: 4, core: 2. Of those that a mesh axis runs over, the one named last changes fastest.
Arguments:
- queries: bfloat16 [2, 4096, 4096], P(None, 'ctx', 'head'), may hold values from -20 to 20
- keys: bfloat16 [2, 4096, 4096], P(None, 'ctx', 'head'), may hold values from -20 to 20
- values: bfloat16 [2, 4096, 4096], P(None, 'ctx', 'head'), may hold values from -6 to 6
- token_rates: float32 [2, 4096, 8], P(None, 'ctx', 'head'), may hold values from 0.05 to 1
- fast_init: float32 [3, 8, 512, 512], P(None, 'head'), may hold values from -0.25 to 0.25
- out_gain: float32 [4096], P('head'), may hold values from 0.5 to 1.5
- out_weight: bfloat16 [4096, 4096], P('head'), may hold values from -0.09375 to 0.09375
Outputs:
- layer_out: bfloat16 [2, 4096, 4096], P(None, ('ctx', 'head'))
- fast_final: float32 [3, 8, 512, 512], P(None, 'head')
All inputs are finite; a program needn't handle non-finite values.
Results may differ from a plain program's by a relative error of at most 0.022.
Values may be sent and summed in bfloat16 or wider, within the bound.
No kernel may reach another device: no remote copies, remote signals or barrier semaphores. Data moves between devices by JAX's collectives and lax.ppermute only.
A program may use at most 192 MiB of HBM per device.

v0:
```python
import jax
import jax.numpy as jnp
from jax import lax
from jax.sharding import PartitionSpec as P

AH = 128
NS_ITERS = 2


coef_a = 3.4445
coef_b = -4.775
coef_c = 2.0315


def shifted(block, axis, distance):
    devices = range(lax.axis_size(axis))
    route = [((i - distance) % len(devices), i) for i in devices]
    return lax.ppermute(block, axis, route)


def head_norm(inputs):
    return inputs / jnp.sqrt(jnp.mean(inputs * inputs, axis=-1, keepdims=True) + 1e-06)


def renorm(previous, fresh):
    target = jnp.sqrt(jnp.mean(previous * previous, axis=-1, keepdims=True) + 1e-06)
    actual = jnp.sqrt(jnp.mean(fresh * fresh, axis=-1, keepdims=True) + 1e-06)
    return fresh * target / actual


def newton_turn(ortho, gram):
    gram_bf = gram.astype(jnp.bfloat16)
    square = jnp.einsum("mhij,mhjk->mhik", gram_bf, gram_bf, preferred_element_type=jnp.float32)
    poly = (coef_b * gram_bf.astype(jnp.float32) + coef_c * square).astype(jnp.bfloat16)
    moved = jnp.einsum("rmhi,mhij->rmhj", ortho, poly, preferred_element_type=jnp.float32)
    return (coef_a * ortho.astype(jnp.float32) + moved).astype(jnp.bfloat16)


def fix_wrapped(received, distance, position):
    rolled = jnp.concatenate([jnp.zeros_like(received[:1]), received[:-1]], 0)
    return jnp.where(position < distance, rolled, received)


def shards(queries, keys, values, token_rates, fast_init, out_gain, out_weight):
    spans, tok, features = queries.shape
    per_dev = fast_init.shape[1]
    width = fast_init.shape[2]
    att_heads = features // AH
    position = lax.axis_index("ctx")
    far_keys = []
    far_values = []
    carried = (keys, values)
    for distance in (1, 2, 3, 4):
        carried = shifted((carried[0], carried[1]), "ctx", 1)
        far_keys.insert(0, fix_wrapped(carried[0], distance, position))
        far_values.insert(0, fix_wrapped(carried[1], distance, position))
    window_keys = jnp.concatenate(far_keys + [keys], 1)
    window_values = jnp.concatenate(far_values + [values], 1)
    scale = AH ** (-0.5)
    query_pos = jnp.arange(tok, dtype=jnp.int32)[:, None]
    key_pos = jnp.arange(5 * tok, dtype=jnp.int32)[None, :]
    distance_pos = query_pos + 4 * tok - key_pos
    in_window = (distance_pos >= 0) & (distance_pos < 4 * tok)
    key_shard = 4 - key_pos // tok
    gain = out_gain.reshape(per_dev, width)
    state = fast_init
    mixed_all = []
    for span in range(spans):
        valid = in_window
        if span == 0:
            valid = valid & jnp.logical_not(position < key_shard)
        query_heads = queries[span].reshape(tok, att_heads, AH)
        key_heads = window_keys[span].reshape(5 * tok, att_heads, AH)
        value_heads = window_values[span].reshape(5 * tok, att_heads, AH)
        scores = (
            jnp.einsum("qnd,knd->nqk", query_heads, key_heads, preferred_element_type=jnp.float32)
            * scale
        )
        scores = jnp.where(valid[None], scores, -1e30)
        largest = jnp.max(scores, axis=-1, keepdims=True)
        expon = jnp.exp(scores - largest)
        probs = (expon / jnp.sum(expon, axis=-1, keepdims=True)).astype(jnp.bfloat16)
        attn = jnp.einsum(
            "nqk,knd->qnd", probs, value_heads, preferred_element_type=jnp.float32
        ).reshape(tok, features)
        query_norm = head_norm(
            queries[span].reshape(tok, per_dev, width).astype(jnp.float32)
        ).astype(jnp.bfloat16)
        key_norm = head_norm(keys[span].reshape(tok, per_dev, width).astype(jnp.float32)).astype(
            jnp.bfloat16
        )
        value_own = values[span].reshape(tok, per_dev, width)
        weights_bf = state.astype(jnp.bfloat16)
        q_first = jnp.einsum(
            "shd,hde->she", query_norm, weights_bf[0], preferred_element_type=jnp.float32
        )
        q_third = jnp.einsum(
            "shd,hde->she", query_norm, weights_bf[1], preferred_element_type=jnp.float32
        )
        query_hidden = (q_first * jax.nn.sigmoid(q_first) * q_third).astype(jnp.bfloat16)
        fast_out = jnp.einsum(
            "she,hed->shd", query_hidden, weights_bf[2], preferred_element_type=jnp.float32
        )
        first = jnp.einsum(
            "shd,hde->she", key_norm, weights_bf[0], preferred_element_type=jnp.float32
        )
        third = jnp.einsum(
            "shd,hde->she", key_norm, weights_bf[1], preferred_element_type=jnp.float32
        )
        sigma = jax.nn.sigmoid(first)
        key_hidden = (first * sigma * third).astype(jnp.bfloat16)
        pull = (-token_rates[span][:, :, None] * value_own.astype(jnp.float32)).astype(jnp.bfloat16)
        back = jnp.einsum("shd,hed->she", pull, weights_bf[2], preferred_element_type=jnp.float32)
        d_first = (back * third * sigma * (1.0 + first * (1.0 - sigma))).astype(jnp.bfloat16)
        d_third = (back * first * sigma).astype(jnp.bfloat16)
        grad_first = jnp.einsum(
            "shr,she->rhe", key_norm, d_first, preferred_element_type=jnp.float32
        )
        grad_third = jnp.einsum(
            "shr,she->rhe", key_norm, d_third, preferred_element_type=jnp.float32
        )
        grad_down = jnp.einsum("shr,shd->rhd", key_hidden, pull, preferred_element_type=jnp.float32)
        grad_rows = lax.psum_scatter(
            jnp.stack([grad_first, grad_third, grad_down], 1).astype(jnp.bfloat16),
            "ctx",
            scatter_dimension=0,
            tiled=True,
        ).astype(jnp.float32)
        squares = lax.psum(jnp.sum(grad_rows * grad_rows, axis=(0, 3)), "ctx")
        ortho_rows = (grad_rows * lax.rsqrt(squares + 1e-06)[None, :, :, None]).astype(jnp.bfloat16)
        ortho = lax.all_gather(ortho_rows, "ctx", axis=0, tiled=True)
        for turn in range(NS_ITERS):
            gram = jnp.einsum("rmhi,rmhj->mhij", ortho, ortho, preferred_element_type=jnp.float32)
            ortho = newton_turn(ortho, gram)
        ortho_mats = jnp.transpose(ortho, (1, 2, 0, 3)).astype(jnp.float32)
        state = renorm(state, state - ortho_mats)
        normed = head_norm(fast_out) * gain
        mixed_all.append((normed.reshape(tok, features) + attn).astype(jnp.bfloat16))
    combined = jnp.stack(mixed_all, 0)
    product = jnp.einsum("ctd,de->tce", combined, out_weight, preferred_element_type=jnp.float32)
    summed = lax.psum_scatter(
        product.astype(jnp.bfloat16), "head", scatter_dimension=0, tiled=True
    ).astype(jnp.float32)
    layer_out = jnp.transpose(summed, (1, 0, 2)).astype(jnp.bfloat16)
    return (layer_out, state)


def solution(mesh):
    placed = (
        P(None, "ctx", "head"),
        P(None, "ctx", "head"),
        P(None, "ctx", "head"),
        P(None, "ctx", "head"),
        P(None, "head", None, None),
        P("head"),
        P("head", None),
    )
    return jax.shard_map(
        shards,
        mesh=mesh,
        in_specs=placed,
        out_specs=(P(None, ("ctx", "head"), None), P(None, "head", None, None)),
        check_vma=False,
    )
```

profile of v0, /device:TPU:0, one launch (start us, length us, event | category | flops | bytes accessed | tf_op | source)
XLA Modules:
  0.0 681.4 jit_solution(7425545014707483364)
XLA Ops:
  39.8 8.7 %copy.313 = bf16[512,3,2,512]{3,2,1,0:T(2,128)(2,1)} copy(bf16[512,3,2,512]{0,3,2,1:T(8,128)(2,1)} %pad_maximum_fusion) | data formatting | bytes 6291456 | tf_op jit(solution)/shard_map/stack | solution.py:124
  56.9 80.5 %all-reduce.13.cloned.1.call-done = bf16[512,3,2,512]{3,2,1,0:T(2,128)(2,1)} async-done(((bf16[512,3,2,512]{3,2,1,0:T(2,128)(2,1)}), bf16[512,3,2,512]{3,2,1,0:T(2,128)(2,1)}) %all-reduce.13.cloned.1.call-update) | async-done | bytes 3145744
  138.9 12.9 %psum.14 = f32[3,2]{1,0:T(4,128)S(1)} all-reduce(f32[3,2]{1,0:T(4,128)S(1)} %fusion.124), channel_id=1, replica_groups=mesh['head'=4,'ctx'=8] {'ctx'}, use_global_device_ids=true, to_apply=%region_7.8 | all-reduce | flops 6 | bytes 48 | tf_op jit(solution)/shard_map/psum | solution.py:129
  180.2 19.5 %collective-permute-done.1 = bf16[2,512,1024]{1,2,0:T(8,128)(2,1)} collective-permute-done((bf16[2,512,1024]{1,2,0:T(8,128)(2,1)}, bf16[2,512,1024]{1,2,0:T(8,128)(2,1)}, u32[]{:S(2)}, u32[]{:S(2)}) %collective-permute-start.1) | collective-permute-done | bytes 2097184 | tf_op jit(solution)/shard_map/ppermute | solution.py:18
  199.8 22.5 %collective-permute-done.5 = bf16[2,512,1024]{1,2,0:T(8,128)(2,1)} collective-permute-done((bf16[2,512,1024]{1,2,0:T(8,128)(2,1)}, bf16[2,512,1024]{1,2,0:T(8,128)(2,1)}, u32[]{:S(2)}, u32[]{:S(2)}) %collective-permute-start.5) | collective-permute-done | bytes 2097184 | tf_op jit(solution)/shard_map/ppermute | solution.py:18
  247.0 20.2 %collective-permute-done.6 = bf16[2,512,1024]{1,2,0:T(8,128)(2,1)} collective-permute-done((bf16[2,512,1024]{1,2,0:T(8,128)(2,1)}, bf16[2,512,1024]{1,2,0:T(8,128)(2,1)}, u32[]{:S(2)}, u32[]{:S(2)}) %collective-permute-start.6) | collective-permute-done | bytes 2097184 | tf_op jit(solution)/shard_map/ppermute | solution.py:18
  269.4 8.9 %copy.314 = bf16[512,3,2,512]{0,3,2,1:T(8,128)(2,1)} copy(bf16[512,3,2,512]{3,2,1,0:T(2,128)(2,1)} %all-gather.3.cloned.1.call-done) | data formatting | bytes 6291456 | tf_op jit(solution)/shard_map/all_gather | solution.py:131
  284.7 11.2 %fusion.19 = bf16[512,3,2,512]{0,3,2,1:T(8,128)(2,1)} fusion(bf16[512,3,2,512]{0,3,2,1:T(8,128)(2,1)} %copy.314, bf16[3,2,512,512]{3,2,1,0:T(8,128)(2,1)} %fusion.176), kind=kOutput, calls=%fused_computation.30 | convolution fusion | flops 3235381248 | bytes 9437184 | tf_op jit(solution)/shard_map/rmhi,mhij->rmhj/dot_general | solution.py:35
  302.3 13.2 %multiply_reduce_fusion.2 = (f32[3,2,512]{2,1,0:T(2,128)S(1)}, bf16[512,3,2,512]{0,3,2,1:T(8,128)(2,1)}) fusion(f32[3,2,512,512]{2,3,1,0:T(8,128)} %copy.322, bf16[512,3,2,512]{0,3,2,1:T(8,128)(2,1)} %fusion.19, bf16[3,2,512,512]{3,2,1,0:T(8,128)(2,1)} %fusion.177), kind=kOutput, calls=%fused_computation.36 | convolution fusion | flops 3241669632 | bytes 15740928 | tf_op jit(solution)/shard_map/rmhi,mhij->rmhj/dot_general | solution.py:35
  328.9 8.7 %copy.345 = bf16[512,3,2,512]{3,2,1,0:T(2,128)(2,1)} copy(bf16[512,3,2,512]{0,3,2,1:T(8,128)(2,1)} %pad_maximum_fusion.1) | data formatting | bytes 6291456 | tf_op jit(solution)/shard_map/stack | solution.py:124
  376.5 8.8 %fusion.166 = (bf16[1,2560,1024]{1,2,0:T(8,128)(2,1)}, bf16[1,2560,1024]{1,2,0:T(8,128)(2,1)}) fusion(bf16[2,2560,1024]{1,2,0:T(8,128)(2,1)} %constant_dynamic-update-slice_fusion.1), kind=kLoop, calls=%fused_computation.240 | loop fusion | bytes 20971520 | tf_op jit(solution)/shard_map/slice | solution.py:73
  385.4 8.8 %fusion.167 = (bf16[1,2560,1024]{1,2,0:T(8,128)(2,1)}, bf16[1,2560,1024]{1,2,0:T(8,128)(2,1)}) fusion(bf16[2,2560,1024]{1,2,0:T(8,128)(2,1)} %copy-done), kind=kLoop, calls=%fused_computation.241 | loop fusion | bytes 20971520 | tf_op jit(solution)/shard_map/slice | solution.py:74
  394.2 24.0 %fusion.174 = (f32[8,512]{1,0:T(8,128)S(1)}, f32[8,512,2560]{1,2,0:T(8,128)}) fusion(pred[512,2560]{0,1:T(8,128)(4,1)S(1)} %copy-done.27, bf16[2560,8,128]{0,2,1:T(8,128)(2,1)} %bitcast.351, bf16[512,8,128]{0,2,1:T(8,128)(2,1)S(1)} %bitcast.360), kind=kOutput, calls=%fused_computation.244 | convolution fusion | flops 2726300160 | bytes 49561600 | tf_op jit(solution)/shard_map/sub | solution.py:81
  418.2 17.8 %fusion.11 = f32[8,128,512]{2,1,0:T(8,128)} fusion(bf16[2560,8,128]{0,2,1:T(8,128)(2,1)} %bitcast.352, f32[8,512,2560]{1,2,0:T(8,128)} %get-tuple-element.41, f32[8,512]{1,0:T(8,128)S(1)} %get-tuple-element.40), kind=kOutput, calls=%fused_computation.17 | convolution fusion | flops 2705326080 | bytes 49299456 | tf_op jit(solution)/shard_map/nqk,knd->qnd/dot_general | solution.py:83
  437.6 23.9 %fusion.175 = (f32[8,512]{1,0:T(8,128)S(1)}, f32[8,512,2560]{1,2,0:T(8,128)}) fusion(pred[512,2560]{0,1:T(8,128)(4,1)S(1)} %copy-done.26, bf16[2560,8,128]{0,2,1:T(8,128)(2,1)} %bitcast.350, bf16[512,8,128]{0,2,1:T(8,128)(2,1)S(1)} %bitcast.356), kind=kOutput, calls=%fused_computation.245 | convolution fusion | flops 2726300160 | bytes 49561600 | tf_op jit(solution)/shard_map/sub | solution.py:81
  461.5 25.5 %psum.15 = f32[3,2]{1,0:T(4,128)S(1)} all-reduce(f32[3,2]{1,0:T(4,128)S(1)} %fusion.126), channel_id=1, replica_groups=mesh['head'=4,'ctx'=8] {'ctx'}, use_global_device_ids=true, to_apply=%region_18.19 | all-reduce | flops 6 | bytes 48 | tf_op jit(solution)/shard_map/psum | solution.py:129
  489.2 18.2 %fusion.10 = f32[8,128,512]{2,1,0:T(8,128)} fusion(bf16[2560,8,128]{0,2,1:T(8,128)(2,1)} %bitcast.349, f32[8,512,2560]{1,2,0:T(8,128)} %get-tuple-element.43, f32[8,512]{1,0:T(8,128)S(1)} %get-tuple-element.42), kind=kOutput, calls=%fused_computation.16 | convolution fusion | flops 2705326080 | bytes 49299456 | tf_op jit(solution)/shard_map/nqk,knd->qnd/dot_general | solution.py:83
  516.2 14.4 %convert_bitcast_fusion = bf16[512,2,4096]{2,0,1:T(8,128)(2,1)} fusion(bf16[1024,4096]{1,0:T(8,128)(2,1)} %param.13, bf16[1,512,1024]{2,1,0:T(8,128)(2,1)S(1)} %add_convert_fusion.16, bf16[1,512,1024]{2,1,0:T(8,128)(2,1)S(1)} %add_convert_fusion.17), kind=kOutput, calls=%fused_computation.20 | convolution fusion | flops 8595177472 | bytes 18874368 | tf_op jit(solution)/shard_map/ctd,de->tce/dot_general | solution.py:140
  530.7 8.8 %copy.346 = bf16[512,3,2,512]{0,3,2,1:T(8,128)(2,1)} copy(bf16[512,3,2,512]{3,2,1,0:T(2,128)(2,1)} %all-gather.5.cloned.1.call-done) | data formatting | bytes 6291456 | tf_op jit(solution)/shard_map/all_gather | solution.py:131
  545.7 10.9 %fusion.17 = bf16[512,3,2,512]{0,3,2,1:T(8,128)(2,1)} fusion(bf16[512,3,2,512]{0,3,2,1:T(8,128)(2,1)} %copy.346, bf16[3,2,512,512]{3,2,1,0:T(8,128)(2,1)} %fusion.178), kind=kOutput, calls=%fused_computation.25 | convolution fusion | flops 3235381248 | bytes 9437184 | tf_op jit(solution)/shard_map/rmhi,mhij->rmhj/dot_general | solution.py:35
  563.1 17.1 %multiply_reduce_fusion.1 = (f32[3,2,512]{2,1,0:T(2,128)S(1)}, f32[3,2,512]{2,1,0:T(2,128)S(1)}, bf16[512,3,2,512]{0,3,2,1:T(8,128)(2,1)}) fusion(f32[3,2,512]{2,1,0:T(2,128)S(1)} %copy-done.29, f32[3,2,512]{2,1,0:T(2,128)S(1)} %copy-done.31, f32[3,2,512,512]{2,3,1,0:T(8,128)} %copy.322, bf16[512,3,2,512]{0,3,2,1:T(8,128)(2,1)} %get-tuple-element.37, ...), kind=kOutput, calls=%fused_computation.33 | convolution fusion | flops 3251103744 | bytes 18923520 | tf_op jit(solution)/shard_map/rmhi,mhij->rmhj/dot_general | solution.py:35
  580.2 7.3 %multiply_divide_fusion = f32[3,2,512,512]{2,3,1,0:T(8,128)} fusion(bf16[512,3,2,512]{0,3,2,1:T(8,128)(2,1)} %get-tuple-element.44, f32[3,2,512]{2,1,0:T(2,128)S(1)} %add_sqrt_fusion, f32[3,2,512]{2,1,0:T(2,128)S(1)} %add_sqrt_fusion.1, f32[3,2,512]{2,1,0:T(2,128)S(1)} %copy-done.29, f32[3,2,512]{2,1,0:T(2,128)S(1)} %copy-done.31, ...), kind=kLoop, calls=%fused_computation.32 | loop fusion | flops 12582912 | bytes 18923520 | tf_op jit(solution)/shard_map/div | solution.py:28
  587.5 6.7 copy.354
  594.2 80.2 %reduce-scatter.2.cloned.1.call-done = bf16[128,2,4096]{2,0,1:T(8,128)(2,1)} async-done(((bf16[512,2,4096]{2,0,1:T(8,128)(2,1)}), bf16[128,2,4096]{2,0,1:T(8,128)(2,1)}) %reduce-scatter.2.cloned.1.call-update) | async-done | bytes 2097168 | tf_op jit(solution)/shard_map/reduce_scatter | solution.py:141
  (183 shorter events, 187.3 us)
Async XLA Ops:
  7.2 130.2 %all-reduce.13.cloned.1.call-start = ((), (), s32[]{:S(2)}) async-start(), calls=%async_computation.4 | async-start | bytes 6291456
  14.0 5.6 copy-start.7
  48.5 7.1 %copy-start.34 = (u32[32]{0:T(128)S(1)}, u32[32]{0:T(128)}, u32[]{:S(2)}) copy-start(u32[32]{0:T(128)} %constant.89) | copy-start | bytes 388
  48.5 220.9 %all-gather.3.cloned.1.call-start = ((), (), s32[]{:S(2)}) async-start(), calls=%async_computation.1 | async-start | bytes 3538944 | tf_op jit(solution)/shard_map/all_gather | solution.py:131
  52.6 109.8 %collective-permute-start = (bf16[2,512,1024]{1,2,0:T(8,128)(2,1)}, bf16[2,512,1024]{1,2,0:T(8,128)(2,1)}, u32[]{:S(2)}, u32[]{:S(2)}) collective-permute-start(bf16[2,512,1024]{1,2,0:T(8,128)(2,1)} %copy.296), channel_id=1, source_target_pairs={{7,0},{0,1},{1,2},{2,3},{3,4},{4,5},{5,6},{6,7},{15,8},{8,9},{9,10... | collective-permute-start | bytes 6291464 | tf_op jit(solution)/shard_map/ppermute | solution.py:18
  53.0 109.3 %collective-permute-start.4 = (bf16[2,512,1024]{1,2,0:T(8,128)(2,1)S(1)}, bf16[2,512,1024]{1,2,0:T(8,128)(2,1)}, u32[]{:S(2)}, u32[]{:S(2)}) collective-permute-start(bf16[2,512,1024]{1,2,0:T(8,128)(2,1)S(1)} %copy.298), channel_id=1, source_target_pairs={{7,0},{0,1},{1,2},{2,3},{3,4},{4,5},{5,6},{6,7},{15,8},{8,9},{9,10... | collective-permute-start | bytes 6291464 | tf_op jit(solution)/shard_map/ppermute | solution.py:18
  154.0 282.0 %all-reduce.15.cloned.1.call-start = ((), (), s32[]{:S(2)}) async-start(), calls=%async_computation.5 | async-start | bytes 6291456
  154.0 6.6 copy-start.33
  162.3 37.4 %collective-permute-start.1 = (bf16[2,512,1024]{1,2,0:T(8,128)(2,1)}, bf16[2,512,1024]{1,2,0:T(8,128)(2,1)}, u32[]{:S(2)}, u32[]{:S(2)}) collective-permute-start(bf16[2,512,1024]{1,2,0:T(8,128)(2,1)} %collective-permute-done), channel_id=1, source_target_pairs={{7,0},{0,1},{1,2},{2,3},{3,4},{4,5},{5,6},{6,7},{15,8},{8,9},{9,10... | collective-permute-start | bytes 6291464 | tf_op jit(solution)/shard_map/ppermute | solution.py:18
  162.4 59.9 %collective-permute-start.5 = (bf16[2,512,1024]{1,2,0:T(8,128)(2,1)}, bf16[2,512,1024]{1,2,0:T(8,128)(2,1)}, u32[]{:S(2)}, u32[]{:S(2)}) collective-permute-start(bf16[2,512,1024]{1,2,0:T(8,128)(2,1)} %collective-permute-done.4), channel_id=1, source_target_pairs={{7,0},{0,1},{1,2},{2,3},{3,4},{4,5},{5,6},{6,7},{15,8},{8,9},{9,10... | collective-permute-start | bytes 6291464 | tf_op jit(solution)/shard_map/ppermute | solution.py:18
  176.8 45.4 %copy-start.14 = (bf16[1,512,1024]{1,2,0:T(8,128)(2,1)S(1)}, bf16[1,512,1024]{1,2,0:T(8,128)(2,1)}, u32[]{:S(2)}) copy-start(bf16[1,512,1024]{1,2,0:T(8,128)(2,1)} %copy.390) | copy-start | bytes 3145732
  199.8 44.9 %collective-permute-start.2 = (bf16[2,512,1024]{1,2,0:T(8,128)(2,1)}, bf16[2,512,1024]{1,2,0:T(8,128)(2,1)}, u32[]{:S(2)}, u32[]{:S(2)}) collective-permute-start(bf16[2,512,1024]{1,2,0:T(8,128)(2,1)} %collective-permute-done.1), channel_id=1, source_target_pairs={{7,0},{0,1},{1,2},{2,3},{3,4},{4,5},{5,6},{6,7},{15,8},{8,9},{9,10... | collective-permute-start | bytes 6291464 | tf_op jit(solution)/shard_map/ppermute | solution.py:18
  222.2 44.9 %collective-permute-start.6 = (bf16[2,512,1024]{1,2,0:T(8,128)(2,1)}, bf16[2,512,1024]{1,2,0:T(8,128)(2,1)}, u32[]{:S(2)}, u32[]{:S(2)}) collective-permute-start(bf16[2,512,1024]{1,2,0:T(8,128)(2,1)} %collective-permute-done.5), channel_id=1, source_target_pairs={{7,0},{0,1},{1,2},{2,3},{3,4},{4,5},{5,6},{6,7},{15,8},{8,9},{9,10... | collective-permute-start | bytes 6291464 | tf_op jit(solution)/shard_map/ppermute | solution.py:18
  247.0 110.9 %collective-permute-start.3 = (bf16[2,512,1024]{1,2,0:T(8,128)(2,1)}, bf16[2,512,1024]{1,2,0:T(8,128)(2,1)}, u32[]{:S(2)}, u32[]{:S(2)}) collective-permute-start(bf16[2,512,1024]{1,2,0:T(8,128)(2,1)} %collective-permute-done.2), channel_id=1, source_target_pairs={{7,0},{0,1},{1,2},{2,3},{3,4},{4,5},{5,6},{6,7},{15,8},{8,9},{9,10... | collective-permute-start | bytes 6291464 | tf_op jit(solution)/shard_map/ppermute | solution.py:18
  269.4 89.8 %collective-permute-start.7 = (bf16[2,512,1024]{1,2,0:T(8,128)(2,1)}, bf16[2,512,1024]{1,2,0:T(8,128)(2,1)}, u32[]{:S(2)}, u32[]{:S(2)}) collective-permute-start(bf16[2,512,1024]{1,2,0:T(8,128)(2,1)} %collective-permute-done.6), channel_id=1, source_target_pairs={{7,0},{0,1},{1,2},{2,3},{3,4},{4,5},{5,6},{6,7},{15,8},{8,9},{9,10... | collective-permute-start | bytes 6291464 | tf_op jit(solution)/shard_map/ppermute | solution.py:18
  337.7 193.0 %all-gather.5.cloned.1.call-start = ((), (), s32[]{:S(2)}) async-start(), calls=%async_computation.3 | async-start | bytes 3538944 | tf_op jit(solution)/shard_map/all_gather | solution.py:131
  367.3 5.8 copy-start
  385.4 8.8 %copy-start.27 = (pred[512,2560]{0,1:T(8,128)(4,1)S(1)}, pred[512,2560]{0,1:T(8,128)(4,1)}, u32[]{:S(2)}) copy-start(pred[512,2560]{0,1:T(8,128)(4,1)} %get-tuple-element.33) | copy-start | bytes 3932164
  418.2 19.4 %copy-start.15 = (bf16[1,512,1024]{1,2,0:T(8,128)(2,1)S(1)}, bf16[1,512,1024]{1,2,0:T(8,128)(2,1)}, u32[]{:S(2)}) copy-start(bf16[1,512,1024]{1,2,0:T(8,128)(2,1)} %copy.390) | copy-start | bytes 3145732
  418.2 19.4 %copy-start.26 = (pred[512,2560]{0,1:T(8,128)(4,1)S(1)}, pred[512,2560]{0,1:T(8,128)(4,1)}, u32[]{:S(2)}) copy-start(pred[512,2560]{0,1:T(8,128)(4,1)} %get-tuple-element.32) | copy-start | bytes 3932164
  489.1 185.2 %reduce-scatter.2.cloned.1.call-start = ((), (), s32[]{:S(2)}) async-start(), calls=%async_computation.2 | async-start | bytes 10485760 | tf_op jit(solution)/shard_map/reduce_scatter | solution.py:141
  489.2 18.2 %copy-start.23 = (f32[8,128,512]{2,1,0:T(8,128)S(1)}, f32[8,128,512]{2,1,0:T(8,128)}, u32[]{:S(2)}) copy-start(f32[8,128,512]{2,1,0:T(8,128)} %fusion.11) | copy-start | bytes 6291460
  556.6 6.4 copy-start.29
  556.6 6.4 copy-start.31
  (24 other events, 62.6 us)
Sparse Core Ops, SparseCore 0:
  48.7 88.6 all-reduce.12
  154.1 38.8 all-gather.2
  337.8 70.6 all-reduce.14
  489.2 31.4 all-gather.4
  530.7 143.5 reduce-scatter.1
where the time goes:
time: 691 us; the launch traced here: 681 us
  waiting for transfers between devices  226 us (33%)
  matrix products  211 us (31%)
  local copies, waits for them, and re-layouts  129 us (19%)
  other arithmetic  58.5 us (8%)
  blocking collectives  38.4 us (6%)
  between operations  15.4 us (2%)
    unnamed x7, waiting for transfers between devices  80.5 us
    reduce_scatter x1, waiting for transfers between devices, shards(): lax.psum_scatter(product.astype(jnp.bfloat16), 'head', scatter_dimension=...  80.2 us
    ppermute x8, waiting for transfers between devices, shifted(): return lax.ppermute(block, axis, route)  65.3 us
    dot_general x4, matrix products, newton_turn(): jnp.einsum('rmhi,mhij->rmhj', ortho, poly, preferred_element_type=jnp.flo...  52.4 us
    sub x2, matrix products, shards(): expon = jnp.exp(scores - largest)  47.9 us
    psum x2, blocking collectives, shards(): squares = lax.psum(jnp.sum(grad_rows * grad_rows, axis=(0, 3)), 'ctx')  38.4 us
    dot_general x2, matrix products, shards(): jnp.einsum('nqk,knd->qnd', probs, value_heads, preferred_element_type=jnp...  36 us
    unnamed x77, local copies, waits for them, and re-layouts  33.8 us
  transfers between devices with their start and end apart: 13, of which 6 were waited for; matrix products, arithmetic and copies ran while one was open for 47% of the time, Pallas kernels for 0%

commit v1 on v0

--- a/solution.py
+++ b/solution.py
@@ -1,15 +1,507 @@
+import functools
+
 import jax
 import jax.numpy as jnp
 from jax import lax
+from jax.experimental import pallas as pl
+from jax.experimental.pallas import tpu as pltpu
 from jax.sharding import PartitionSpec as P
 
 AH = 128
 NS_ITERS = 2
+BACK = 4
 
 
 coef_a = 3.4445
 coef_b = -4.775
 coef_c = 2.0315
+LOG2E = 1.4426950408889634
+F32 = jnp.float32
+BF16 = jnp.bfloat16
+NOWHERE = 2**20
+VMEM_BYTES = 56 * 1024 * 1024
+
+
+def swapped(block, mask):
+    devices = range(lax.axis_size("ctx"))
+    return lax.ppermute(block, "ctx", [(i, i ^ mask) for i in devices])
+
+
+def raised(block, step):
+    devices = range(lax.axis_size("ctx") - step)
+    return lax.ppermute(block, "ctx", [(i, i + step) for i in devices])
+
+
+def after(value, *earlier):
+    return lax.optimization_barrier((value,) + earlier)[0]
+
+
+def rms_inverse(inputs):
+    return lax.rsqrt(jnp.mean(inputs * inputs, axis=-1, keepdims=True) + 1e-06)
+
+
+def sigmoid(inputs):
+    return 0.5 * jnp.tanh(0.5 * inputs) + 0.5
+
+
+def dot_nn(left, right):
+    return lax.dot_general(left, right, (((1,), (0,)), ((), ())), preferred_element_type=F32)
+
+
+def dot_nt(left, right):
+    return lax.dot_general(left, right, (((1,), (1,)), ((), ())), preferred_element_type=F32)
+
+
+def dot_tn(left, right):
+    return lax.dot_general(left, right, (((0,), (0,)), ((), ())), preferred_element_type=F32)
+
+
+def params():
+    return pltpu.CompilerParams(vmem_limit_bytes=VMEM_BYTES)
+
+
+def cost(flops, bytes_accessed, transcendentals=0):
+    return pl.CostEstimate(
+        flops=flops, bytes_accessed=bytes_accessed, transcendentals=transcendentals
+    )
+
+
+def in_vmem(count):
+    return [pl.BlockSpec(memory_space=pltpu.VMEM)] * count
+
+
+IN_SMEM = pl.BlockSpec(memory_space=pltpu.SMEM)
+
+
+def token_grads(kv_ref, rate_ref, weight_ref, emit):
+    keys = kv_ref[0].astype(F32)
+    normed = (keys * rms_inverse(keys)).astype(BF16)
+    pull = (-rate_ref[:, :1] * kv_ref[1].astype(F32)).astype(BF16)
+    first = dot_nn(normed, weight_ref[0])
+    third = dot_nn(normed, weight_ref[1])
+    back = dot_nt(pull, weight_ref[2])
+    sigma = sigmoid(first)
+    silu = first * sigma
+    hidden = (silu * third).astype(BF16)
+    d_third = (back * silu).astype(BF16)
+    d_first = (back * third * (sigma * (1.0 + first - silu))).astype(BF16)
+    emit(0, dot_tn(normed, d_first))
+    emit(1, dot_tn(normed, d_third))
+    emit(2, dot_tn(hidden, pull))
+
+
+def grads_first_kernel(kv_ref, rate_ref, weight_ref, out_ref):
+    def emit(index, value):
+        out_ref[index] = value
+
+    token_grads(kv_ref, rate_ref, weight_ref, emit)
+
+
+def grads_second_kernel(core_ref, kv_ref, rate_ref, weight_ref, sum_ref, keep_ref, give_ref, all_ref):
+    half = keep_ref.shape[1]
+    core = core_ref[0]
+
+    def emit(index, value):
+        all_ref[index] = value + sum_ref[index]
+
+    token_grads(kv_ref, rate_ref, weight_ref, emit)
+    for index in range(all_ref.shape[0]):
+        mine = pl.ds(pl.multiple_of(core * half, half), half)
+        other = pl.ds(pl.multiple_of((1 - core) * half, half), half)
+        keep_ref[index] = all_ref[index, mine, :].astype(BF16)
+        give_ref[index] = all_ref[index, other, :].astype(BF16)
+
+
+def grads_first(kv, rates, weights):
+    tok, width = kv.shape[1:]
+    flops = 12 * tok * width * width
+    return pl.pallas_call(
+        grads_first_kernel,
+        out_shape=jax.ShapeDtypeStruct((3, width, width), F32),
+        in_specs=in_vmem(3),
+        out_specs=in_vmem(1)[0],
+        compiler_params=params(),
+        cost_estimate=cost(flops, 16 * width * width),
+        name="grads_first",
+    )(kv, rates, weights)
+
+
+def grads_second(core, kv, rates, weights, partial):
+    tok, width = kv.shape[1:]
+    flops = 12 * tok * width * width
+    half = jax.ShapeDtypeStruct((3, width // 2, width), BF16)
+    return pl.pallas_call(
+        grads_second_kernel,
+        out_shape=(half, half),
+        in_specs=[IN_SMEM] + in_vmem(4),
+        out_specs=tuple(in_vmem(2)),
+        scratch_shapes=[pltpu.VMEM((3, width, width), F32)],
+        compiler_params=params(),
+        cost_estimate=cost(flops, 28 * width * width),
+        name="grads_second",
+    )(core, kv, rates, weights, partial)
+
+
+def muon_kernel(core_ref, mine_ref, other_ref, *refs, update):
+    if update:
+        state_ref, ortho_ref, half_ref, weight_ref, grad_ref = refs
+    else:
+        ortho_ref, half_ref, grad_ref = refs
+    half = mine_ref.shape[1]
+    core = core_ref[0]
+    mine = pl.ds(pl.multiple_of(core * half, half), half)
+    other = pl.ds(pl.multiple_of((1 - core) * half, half), half)
+    count = mine_ref.shape[0]
+    for index in range(count):
+        grad_ref[index, mine, :] = mine_ref[index].astype(F32)
+        grad_ref[index, other, :] = other_ref[index].astype(F32)
+    ortho = []
+    for index in range(count):
+        grad = grad_ref[index]
+        ortho.append((grad * lax.rsqrt(jnp.sum(grad * grad) + 1e-06)).astype(BF16))
+    for turn in range(NS_ITERS):
+        gram = [dot_tn(mat, mat).astype(BF16) for mat in ortho]
+        poly = [(coef_b * mat.astype(F32) + coef_c * dot_nn(mat, mat)).astype(BF16) for mat in gram]
+        ortho = [
+            (coef_a * mat.astype(F32) + dot_nn(mat, step)).astype(BF16)
+            for mat, step in zip(ortho, poly)
+        ]
+    for index in range(count):
+        ortho_ref[index] = ortho[index]
+        half_ref[index] = ortho_ref[index, mine, :]
+        if update:
+            weight_ref[index] = renorm(state_ref[index, 0], ortho[index].astype(F32)).astype(BF16)
+
+
+def renorm(previous, step):
+    fresh = previous - step
+    target = jnp.sqrt(jnp.mean(previous * previous, axis=-1, keepdims=True) + 1e-06)
+    return fresh * (target * rms_inverse(fresh))
+
+
+def muon(core, mine, other, state=None, side=None):
+    count, half, width = mine.shape
+    whole = jax.ShapeDtypeStruct((count, width, width), BF16)
+    part = jax.ShapeDtypeStruct((count, half, width), BF16)
+    update = state is not None
+    outs = (whole, part, whole) if update else (whole, part)
+    body = functools.partial(muon_kernel, update=update)
+    grid_spec = pltpu.PrefetchScalarGridSpec(
+        num_scalar_prefetch=1,
+        grid=(1,),
+        in_specs=[pl.BlockSpec((count, half, width), lambda i, s: (0, 0, 0))] * 2
+        + (
+            [pl.BlockSpec((count, 1, width, width), lambda i, s: (0, s[1], 0, 0))]
+            if update
+            else []
+        ),
+        out_specs=tuple(pl.BlockSpec(out.shape, lambda i, s: (0, 0, 0)) for out in outs),
+        scratch_shapes=[pltpu.VMEM((count, width, width), F32)],
+    )
+    scalars = jnp.stack([core, core if side is None else side])
+    return pl.pallas_call(
+        body,
+        out_shape=outs,
+        grid_spec=grid_spec,
+        compiler_params=params(),
+        cost_estimate=cost(count * NS_ITERS * 6 * width**3, 12 * width * width),
+        name="muon",
+    )(scalars, mine, other, *((state,) if update else ()))
+
+
+def finish_kernel(scalar_ref, state_ref, *refs):
+    spans = (len(refs) - 1) // 3
+    out_ref = refs[-1]
+    core, side = scalar_ref[0], scalar_ref[1]
+    half = refs[1].shape[1]
+    head = pl.program_id(1)
+
+    def advance(steps):
+        value = state_ref[0, 0]
+        for step in steps:
+            value = renorm(value, step.astype(F32))
+        out_ref[0, 0] = value
+
+    @pl.when(head == side)
+    def _own():
+        advance([refs[3 * span][0] for span in range(spans)])
+
+    @pl.when((head != side) & (core == 0))
+    def _first():
+        advance(
+            [jnp.concatenate([refs[3 * span + 1][0], refs[3 * span + 2][0]], 0) for span in range(spans)]
+        )
+
+    @pl.when((head != side) & (core != 0))
+    def _second():
+        advance(
+            [jnp.concatenate([refs[3 * span + 2][0], refs[3 * span + 1][0]], 0) for span in range(spans)]
+        )
+
+
+def finish(core, side, state, steps):
+    count, heads, width, _ = state.shape
+    half = width // 2
+    specs = []
+    for _ in steps:
+        specs.append(pl.BlockSpec((1, width, width), lambda m, h, s: (m, 0, 0)))
+        specs.append(pl.BlockSpec((1, half, width), lambda m, h, s: (m, 0, 0)))
+        specs.append(pl.BlockSpec((1, half, width), lambda m, h, s: (m, 0, 0)))
+    one = pl.BlockSpec((1, 1, width, width), lambda m, h, s: (m, h, 0, 0))
+    grid_spec = pltpu.PrefetchScalarGridSpec(
+        num_scalar_prefetch=1,
+        grid=(count, heads),
+        in_specs=[one] + specs,
+        out_specs=one,
+    )
+    flat = [array for step in steps for array in step]
+    return pl.pallas_call(
+        finish_kernel,
+        out_shape=jax.ShapeDtypeStruct(state.shape, F32),
+        grid_spec=grid_spec,
+        compiler_params=params(),
+        cost_estimate=cost(20 * state.size, 8 * state.size + 4 * state.size),
+        name="finish",
+    )(jnp.stack([core, side]), state, *flat)
+
+
+def attend_kernel(ids_ref, query_ref, *refs, blocks, start, end):
+    refs = list(refs)
+    kv_refs, refs = refs[:blocks], refs[blocks:]
+    if start:
+        sum_in_ref = top_in_ref = None
+    else:
+        (sum_in_ref, top_in_ref), refs = refs[:2], refs[2:]
+    if end:
+        out_ref, refs = refs[0], refs[1:]
+        sum_ref, top_ref, bias_ref = refs
+    else:
+        sum_ref, top_ref, bias_ref = refs
+    tok = query_ref.shape[1]
+    width = query_ref.shape[2]
+    head = pl.program_id(0)
+    which = pl.program_id(1)
+
+    @pl.when((head == 0) & (which == 0))
+    def _bias():
+        row = lax.broadcasted_iota(jnp.int32, (tok, tok), 0)
+        column = lax.broadcasted_iota(jnp.int32, (tok, tok), 1)
+        bias_ref[0] = jnp.where(column <= row, 0.0, -1e30)
+        bias_ref[1] = jnp.zeros((tok, tok), F32)
+        bias_ref[2] = jnp.where(column > row, 0.0, -1e30)
+
+    if start:
+        sum_ref[...] = jnp.zeros_like(sum_ref)
+        top_ref[...] = jnp.full_like(top_ref, -1e30)
+    else:
+        sum_ref[...] = sum_in_ref[...]
+        top_ref[...] = top_in_ref[...]
+    query = query_ref[0]
+    place = ids_ref[which]
+    ones = jnp.ones((tok, width), BF16)
+    for block in range(blocks):
+        apart = place - ids_ref[2 + block]
+
+        @pl.when((apart >= 0) & (apart <= BACK))
+        def _block(block=block, apart=apart):
+            kind = jnp.where(apart == 0, 0, jnp.where(apart == BACK, 2, 1))
+            values = jnp.concatenate([kv_refs[block][1], ones], 1)
+            rows = tok // 2
+            for part in range(2):
+                span = pl.ds(part * rows, rows)
+                scores = dot_nt(query[part * rows : (part + 1) * rows], kv_refs[block][0])
+                scores = scores * (AH**-0.5 * LOG2E) + bias_ref[kind, span, :]
+                old = top_ref[0, 0, span, :]
+                top = jnp.maximum(old, jnp.max(scores, axis=-1, keepdims=True))
+                weights = jnp.exp2(scores - top[:, :1]).astype(BF16)
+                shrink = jnp.exp2(old - top)
+                fresh = dot_nn(weights, values)
+                sum_ref[0, 0, span, :width] = sum_ref[0, 0, span, :width] * shrink + fresh[:, :width]
+                sum_ref[0, 0, span, width:] = sum_ref[0, 0, span, width:] * shrink + fresh[:, width:]
+                top_ref[0, 0, span, :] = top
+
+    if end:
+        out_ref[0] = (sum_ref[0, 0, :, :width] / sum_ref[0, 0, :, width:]).astype(BF16)
+
+
+def attend(ids, queries, kvs, carry=None, end=False):
+    two, tok, features = queries.shape
+    heads = features // AH
+    blocks = len(kvs)
+    start = carry is None
+    query_spec = pl.BlockSpec((1, tok, AH), lambda h, w, s: (w, 0, h))
+    kv_spec = pl.BlockSpec((2, tok, AH), lambda h, w, s: (0, 0, h))
+    sum_spec = pl.BlockSpec((1, 1, tok, 2 * AH), lambda h, w, s: (h, w, 0, 0))
+    top_spec = pl.BlockSpec((1, 1, tok, AH), lambda h, w, s: (h, w, 0, 0))
+    sum_shape = jax.ShapeDtypeStruct((heads, two, tok, 2 * AH), F32)
+    top_shape = jax.ShapeDtypeStruct((heads, two, tok, AH), F32)
+    scratch = [pltpu.VMEM((3, tok, tok), F32)]
+    if end:
+        outs, out_specs = jax.ShapeDtypeStruct(queries.shape, BF16), query_spec
+        scratch = [
+            pltpu.VMEM((1, 1, tok, 2 * AH), F32),
+            pltpu.VMEM((1, 1, tok, AH), F32),
+        ] + scratch
+    else:
+        outs, out_specs = (sum_shape, top_shape), (sum_spec, top_spec)
+    grid_spec = pltpu.PrefetchScalarGridSpec(
+        num_scalar_prefetch=1,
+        grid=(heads, two),
+        in_specs=[query_spec] + [kv_spec] * blocks + ([] if start else [sum_spec, top_spec]),
+        out_specs=out_specs,
+        scratch_shapes=scratch,
+    )
+    pairs = heads * 5
+    return pl.pallas_call(
+        functools.partial(attend_kernel, blocks=blocks, start=start, end=end),
+        out_shape=outs,
+        grid_spec=grid_spec,
+        compiler_params=params(),
+        cost_estimate=cost(
+            pairs * 8 * tok * tok * AH, blocks * 4 * tok * features, pairs * tok * tok
+        ),
+        name="attend",
+    )(ids, queries, *kvs, *(() if start else carry))
+
+
+def answer_kernel(query_ref, weight_ref, gain_ref, out_ref):
+    query = query_ref[0].astype(F32)
+    normed = (query * rms_inverse(query)).astype(BF16)
+    first = dot_nn(normed, weight_ref[0])
+    third = dot_nn(normed, weight_ref[1])
+    hidden = (first * sigmoid(first) * third).astype(BF16)
+    answer = dot_nn(hidden, weight_ref[2])
+    out_ref[0] = answer * rms_inverse(answer) * gain_ref[...]
+
+
+def answer(queries, weights, gain):
+    two, tok, width = queries.shape
+    block = pl.BlockSpec((1, tok, width), lambda w: (w, 0, 0))
+    return pl.pallas_call(
+        answer_kernel,
+        out_shape=jax.ShapeDtypeStruct(queries.shape, F32),
+        grid=(two,),
+        in_specs=[
+            block,
+            pl.BlockSpec(weights.shape, lambda w: (0, 0, 0)),
+            pl.BlockSpec((1, width), lambda w: (0, 0)),
+        ],
+        out_specs=block,
+        compiler_params=params(),
+        cost_estimate=cost(two * 6 * tok * width * width, 10 * tok * width),
+        name="answer",
+    )(queries, weights, gain)
+
+
+def shards(queries, keys, values, token_rates, fast_init, out_gain, out_weight):
+    spans, tok, features = queries.shape
+    width = fast_init.shape[2]
+    position = lax.axis_index("ctx")
+    around = lax.axis_size("ctx")
+    upper = around // 2
+    core = position % 2
+    side = (position // 2) % 2
+    far = position // upper
+    here = side == 0
+
+    def keep(array):
+        return jnp.where(here, array[..., :width], array[..., width:])
+
+    def give(array):
+        return jnp.where(here, array[..., width:], array[..., :width])
+
+    gain = keep(out_gain[None, :])
+    rates_own = jnp.where(here, token_rates[..., 0], token_rates[..., 1])
+    rates_away = jnp.where(here, token_rates[..., 1], token_rates[..., 0])
+    rates_got = swapped(rates_away, 2)
+
+    def column(rates):
+        return jnp.broadcast_to(rates[:, None], (tok, 128))
+
+    kv_own = [jnp.stack([keep(keys[span]), keep(values[span])]) for span in range(spans)]
+    kv_away = [jnp.stack([give(keys[span]), give(values[span])]) for span in range(spans)]
+    weights = jnp.where(here, fast_init[:, 0], fast_init[:, 1]).astype(BF16)
+
+    kv_got = [swapped(kv_away[0], 2)]
+    query_got = [swapped(after(give(queries[0]), kv_got[0]), 2)]
+    kv_got.append(swapped(after(kv_away[1], query_got[0]), 2))
+    query_got.append(swapped(after(give(queries[1]), kv_got[1]), 2))
+    query_both = [jnp.stack([keep(queries[span]), query_got[span]]) for span in range(spans)]
+
+    far_own = [swapped(kv_own[0], upper)]
+    far_got = [swapped(after(kv_got[0], far_own[0]), upper)]
+    near = [[kv_own[0], kv_got[0], swapped(kv_own[0], 1), swapped(kv_got[0], 1)]]
+    fars = [[far_own[0], far_got[0], swapped(far_own[0], 1), swapped(far_got[0], 1)]]
+
+    own_place = 2 * side + core
+    got_place = 2 * (1 - side) + core
+    own_pair = 2 * side + 1 - core
+    got_pair = 2 * (1 - side) + 1 - core
+    places = jnp.stack([own_place, got_place, own_pair, got_pair]).astype(jnp.int32)
+
+    def ids(span, *bases):
+        mine = span * around + far * upper + places[:2]
+        return jnp.concatenate([mine] + [base + places for base in bases]).astype(jnp.int32)
+
+    partial = grads_first(kv_own[0], column(rates_own[0]), weights)
+    sums_keep, sums_give = grads_second(
+        core[None].astype(jnp.int32), kv_got[0], column(rates_got[0]), weights, partial
+    )
+    steps = []
+    mixed_full = []
+    products = []
+    for span in range(spans):
+        base = span * around
+        chip = (sums_keep.astype(F32) + swapped(sums_give, 1).astype(F32)).astype(BF16)
+        total = (chip.astype(F32) + swapped(after(chip, far_got[span]), upper).astype(F32)).astype(BF16)
+        pair = swapped(total, 1)
+        if span + 1 < spans:
+            ortho, ortho_half, next_weights = muon(core, total, pair, fast_init, side)
+        else:
+            ortho, ortho_half = muon(core, total, pair)
+        carry = attend(ids(span, base + far * upper), query_both[span], near[span])
+        if span == 0:
+            late = jnp.where(far == 0, NOWHERE, base)
+            attn = attend(ids(span, late), query_both[span], fars[span], carry, True)
+        else:
+            early = jnp.where(far == 0, base - upper, NOWHERE)
+            late = jnp.where(far == 0, NOWHERE, base)
+            attn = attend(
+                ids(span, early, late), query_both[span], fars[span - 1] + fars[span], carry, True
+            )
+        fast = answer(query_both[span], weights, gain)
+        mixed = (fast + attn.astype(F32)).astype(BF16)
+        returned = swapped(mixed[1], 2)
+        full = jnp.concatenate(
+            [jnp.where(here, mixed[0], returned), jnp.where(here, returned, mixed[0])], 1
+        )
+        product = jnp.dot(full, out_weight, preferred_element_type=F32).astype(BF16)
+        products.append(lax.psum_scatter(product, "head", scatter_dimension=0, tiled=True))
+        if span + 1 < spans:
+            weights = next_weights
+            following = span + 1
+            partial = grads_first(kv_own[following], column(rates_own[following]), weights)
+            sums_keep, sums_give = grads_second(
+                core[None].astype(jnp.int32),
+                kv_got[following],
+                column(rates_got[following]),
+                weights,
+                partial,
+            )
+            far_own.append(raised(after(kv_own[following], far_got[span]), upper))
+            far_got.append(raised(after(kv_got[following], far_own[following]), upper))
+            near.append(
+                [kv_own[following], kv_got[following]]
+                + [swapped(kv_own[following], 1), swapped(kv_got[following], 1)]
+            )
+            fars.append(
+                [far_own[following], far_got[following]]
+                + [swapped(far_own[following], 1), swapped(far_got[following], 1)]
+            )
+        away = swapped(after(ortho_half, query_got[-1]), 2)
+        steps.append((ortho, away, swapped(away, 1)))
+    state = finish(core, side, fast_init, steps)
+    return (jnp.stack(products, 0), state)
 
 
 def shifted(block, axis, distance):
@@ -22,7 +514,7 @@
     return inputs / jnp.sqrt(jnp.mean(inputs * inputs, axis=-1, keepdims=True) + 1e-06)
 
 
-def renorm(previous, fresh):
+def renormed(previous, fresh):
     target = jnp.sqrt(jnp.mean(previous * previous, axis=-1, keepdims=True) + 1e-06)
     actual = jnp.sqrt(jnp.mean(fresh * fresh, axis=-1, keepdims=True) + 1e-06)
     return fresh * target / actual
@@ -41,7 +533,7 @@
     return jnp.where(position < distance, rolled, received)
 
 
-def shards(queries, keys, values, token_rates, fast_init, out_gain, out_weight):
+def shards_any(queries, keys, values, token_rates, fast_init, out_gain, out_weight):
     spans, tok, features = queries.shape
     per_dev = fast_init.shape[1]
     width = fast_init.shape[2]
@@ -133,7 +625,7 @@
             gram = jnp.einsum("rmhi,rmhj->mhij", ortho, ortho, preferred_element_type=jnp.float32)
             ortho = newton_turn(ortho, gram)
         ortho_mats = jnp.transpose(ortho, (1, 2, 0, 3)).astype(jnp.float32)
-        state = renorm(state, state - ortho_mats)
+        state = renormed(state, state - ortho_mats)
         normed = head_norm(fast_out) * gain
         mixed_all.append((normed.reshape(tok, features) + attn).astype(jnp.bfloat16))
     combined = jnp.stack(mixed_all, 0)
@@ -143,6 +635,12 @@
     ).astype(jnp.float32)
     layer_out = jnp.transpose(summed, (1, 0, 2)).astype(jnp.bfloat16)
     return (layer_out, state)
+
+
+def plan(queries, keys, values, token_rates, fast_init, out_gain, out_weight):
+    halved = lax.axis_size("ctx") == 2 * BACK and fast_init.shape[1] == 2 and queries.shape[0] == 2
+    chosen = shards if halved else shards_any
+    return chosen(queries, keys, values, token_rates, fast_init, out_gain, out_weight)
 
 
 def solution(mesh):
@@ -156,7 +654,7 @@
         P("head", None),
     )
     return jax.shard_map(
-        shards,
+        plan,
         mesh=mesh,
         in_specs=placed,
         out_specs=(P(None, ("ctx", "head"), None), P(None, "head", None, None)),

time: 691 us -> 425 us (0.62)
  matrix products: 211 us -> 19.7 us
  Pallas kernels: 0 us -> 142 us
  local copies, waits for them, and re-layouts: 129 us -> 14.6 us
  waiting for transfers between devices: 226 us -> 155 us
  starting transfers between devices: 3.54 us -> 54.4 us
  blocking collectives: 38.4 us -> 0 us
  other arithmetic: 58.5 us -> 20.7 us
    dot_general x27 -> x2, matrix products: 163 us -> 19.7 us  [shards(): product = jnp.dot(full, out_weight, preferred_element_type=F32).astype(BF16)]
    pallas_call x0 -> x13, Pallas kernels: none -> 142 us  [the longest x4 74.7 us: attend(): pl.pallas_call(functools.partial(attend_kernel, blocks=blocks, start=star...]
    ppermute x8 -> x29, waiting for transfers between devices: 65.3 us -> 155 us  [the longest x27 129 us: swapped(): return lax.ppermute(block, 'ctx', [(i, i ^ mask) for i in devices])]
    unnamed x7 -> x2, waiting for transfers between devices: 80.5 us -> 0.03 us
    reduce_scatter x1 -> x2, waiting for transfers between devices: 80.2 us -> 0.01 us  [shards(): lax.psum_scatter(product, 'head', scatter_dimension=0, tiled=True)]
    ppermute x8 -> x29, starting transfers between devices: 3.34 us -> 53.8 us  [the longest x27 28.3 us: swapped(): return lax.ppermute(block, 'ctx', [(i, i ^ mask) for i in devices])]
    sub x2 -> x0, matrix products: 47.9 us -> none  [shards(): expon = jnp.exp(scores - largest)]
    psum x2 -> x0, blocking collectives: 38.4 us -> none  [shards(): squares = lax.psum(jnp.sum(grad_rows * grad_rows, axis=(0, 3)), 'ctx')]
  transfers between devices with their start and end apart: 13 -> 31, of which waited for: 6 -> 16; matrix products, arithmetic and copies ran while one was open for 47% -> 7% of each run, Pallas kernels for 0% -> 32%
where the time goes in v1:
time: 425 us; the launch traced here: 421 us
  waiting for transfers between devices  155 us (36%)
  Pallas kernels  142 us (33%)
  starting transfers between devices  54.4 us (13%)
  other arithmetic  20.7 us (5%)
  matrix products  19.7 us (5%)
  between operations  14.7 us (3%)
  local copies, waits for them, and re-layouts  14.6 us (3%)
    ppermute x27, waiting for transfers between devices, swapped(): return lax.ppermute(block, 'ctx', [(i, i ^ mask) for i in devices])  129 us
    pallas_call x4, Pallas kernels, attend(): pl.pallas_call(functools.partial(attend_kernel, blocks=blocks, start=star...  74.7 us
    ppermute x27, starting transfers between devices, swapped(): return lax.ppermute(block, 'ctx', [(i, i ^ mask) for i in devices])  28.3 us
    ppermute x2, waiting for transfers between devices, raised(): return lax.ppermute(block, 'ctx', [(i, i + step) for i in devices])  25.7 us
    ppermute x2, starting transfers between devices, raised(): return lax.ppermute(block, 'ctx', [(i, i + step) for i in devices])  25.5 us
    pallas_call x2, Pallas kernels, muon(): pl.pallas_call(body, out_shape=outs, grid_spec=grid_spec, compiler_params...  21.3 us
    dot_general x2, matrix products, shards(): product = jnp.dot(full, out_weight, preferred_element_type=F32).astype(BF16)  19.7 us
    pallas_call x2, Pallas kernels, grads_second(): pl.pallas_call(grads_second_kernel, out_shape=(half, half), in_specs=[IN_...  13.2 us
  transfers between devices with their start and end apart: 31, of which 16 were waited for; matrix products, arithmetic and copies ran while one was open for 7% of the time, Pallas kernels for 32%

profile of v1, /device:TPU:0, one launch (start us, length us, event | category | flops | bytes accessed | tf_op | source)
XLA Modules:
  0.0 421.2 jit_solution(15602573269785180024)
XLA Ops:
  15.7 20.5 %collective-permute-done.refs_1_.kv_ref = bf16[2,512,512]{2,1,0:T(8,128)(2,1)} collective-permute-done((bf16[2,512,512]{2,1,0:T(8,128)(2,1)S(1)}, bf16[2,512,512]{2,1,0:T(8,128)(2,1)}, u32[]{:S(2)}, u32[]{:S(2)}) %collective-permute-start) | collective-permute-done | bytes 1048608 | tf_op jit(solution)/shard_map/ppermute | solution.py:27
  47.4 15.4 %collective-permute-done.3.refs_1_ = bf16[2,512,512]{2,1,0:T(8,128)(2,1)S(1)} collective-permute-done((bf16[2,512,512]{2,1,0:T(8,128)(2,1)}, bf16[2,512,512]{2,1,0:T(8,128)(2,1)S(1)}, u32[]{:S(2)}, u32[]{:S(2)}) %collective-permute-start.3) | collective-permute-done | bytes 1048608 | tf_op jit(solution)/shard_map/ppermute | solution.py:27
  71.4 19.0 %attend.4 = (f32[4,2,512,256]{3,2,1,0:T(8,128)}, f32[4,2,512,128]{3,2,1,0:T(8,128)}) custom-call(s32[6]{0:T(128)} %get-tuple-element.78.ids_ref, bf16[2,512,512]{2,1,0:T(8,128)(2,1)} %pad_maximum_fusion.2.query_ref, bf16[2,512,512]{2,1,0:T(8,128)(2,1)} %pad_maximum_fusion.3.refs_0_.kv_ref, bf16[2,512,512]{2,1,0:T(8,128)(2,1)} %collective-permute-done.refs_1_.kv_ref, ...), custom_call_target="tpu_custom_call" | custom-call | flops 5368709120 | bytes 4194304 | tf_op jit(solution)/shard_map/attend/pallas_call | solution.py:355
  91.8 9.1 %attend.5 = bf16[2,512,512]{2,1,0:T(8,128)(2,1)} custom-call(s32[6]{0:T(128)} %get-tuple-element.79.ids_ref, bf16[2,512,512]{2,1,0:T(8,128)(2,1)} %pad_maximum_fusion.2.query_ref, bf16[2,512,512]{2,1,0:T(8,128)(2,1)} %collective-permute-done.2.refs_0_, bf16[2,512,512]{2,1,0:T(8,128)(2,1)} %copy-done.14, bf16[2,512,512]{2,1,0:T(8,128)(2,1)} %copy-done.15, ...), custom_call_target="tpu_custom_call" | custom-call | flops 5368709120 | bytes 4194304 | tf_op jit(solution)/shard_map/attend/pallas_call | solution.py:355
  104.4 7.3 %collective-permute-done.8 = bf16[512,512]{1,0:T(8,128)(2,1)S(1)} collective-permute-done((bf16[512,512]{1,0:T(8,128)(2,1)S(1)}, bf16[512,512]{1,0:T(8,128)(2,1)S(1)}, u32[]{:S(2)}, u32[]{:S(2)}) %collective-permute-start.8) | collective-permute-done | bytes 524320 | tf_op jit(solution)/shard_map/ppermute | solution.py:27
  111.8 9.7 %convolution_convert_fusion.1 = bf16[512,4096]{1,0:T(8,128)(2,1)} fusion(bf16[1024,4096]{1,0:T(8,128)(2,1)} %param.13, bf16[512,512]{1,0:T(8,128)(2,1)S(1)} %get-tuple-element.57, bf16[512,512]{1,0:T(8,128)(2,1)S(1)} %get-tuple-element.56), kind=kOutput, calls=%fused_computation.1 | convolution fusion | flops 4299161600 | bytes 13631488 | tf_op jit(solution)/shard_map/dot_general | solution.py:478
  131.4 6.2 %grads_second.2 = (bf16[3,256,512]{2,1,0:T(8,128)(2,1)}, bf16[3,256,512]{2,1,0:T(8,128)(2,1)}) custom-call(s32[1]{0:T(128)} %bitcast.25.core_ref, bf16[2,512,512]{2,1,0:T(8,128)(2,1)} %collective-permute-done.refs_1_.kv_ref, f32[512,128]{1,0:T(8,128)} %broadcast_in_dim.35.rate_ref, bf16[3,512,512]{2,1,0:T(8,128)(2,1)} %fusion.1.weight_ref, ...), custom_call_target="tpu_custom_call" | custom-call | flops 1610612736 | bytes 7340032 | tf_op jit(solution)/shard_map/grads_second/pallas_call | solution.py:133
  144.7 20.1 %collective-permute-start.15 = (bf16[2,512,512]{2,1,0:T(8,128)(2,1)S(1)}, bf16[2,512,512]{2,1,0:T(8,128)(2,1)S(1)}, u32[]{:S(2)}, u32[]{:S(2)}) collective-permute-start(bf16[2,512,512]{2,1,0:T(8,128)(2,1)S(1)} %pad_maximum_fusion.6.refs_0_.kv_ref), channel_id=1, source_target_pairs={{0,4},{1,5},{2,6},{3,7},{8,12},{9,13},{10,14},{11,15},{16,20},{17,... | collective-permute-start | bytes 3145736 | tf_op jit(solution)/shard_map/ppermute | solution.py:32
  168.4 19.9 %collective-permute-done.15.refs_4_ = bf16[2,512,512]{2,1,0:T(8,128)(2,1)S(1)} collective-permute-done((bf16[2,512,512]{2,1,0:T(8,128)(2,1)S(1)}, bf16[2,512,512]{2,1,0:T(8,128)(2,1)S(1)}, u32[]{:S(2)}, u32[]{:S(2)}) %collective-permute-start.15) | collective-permute-done | bytes 1048608 | tf_op jit(solution)/shard_map/ppermute | solution.py:32
  193.6 11.5 %collective-permute-done.13 = bf16[3,256,512]{2,1,0:T(8,128)(2,1)S(1)} collective-permute-done((bf16[3,256,512]{2,1,0:T(8,128)(2,1)S(1)}, bf16[3,256,512]{2,1,0:T(8,128)(2,1)S(1)}, u32[]{:S(2)}, u32[]{:S(2)}) %collective-permute-start.13) | collective-permute-done | bytes 786464 | tf_op jit(solution)/shard_map/ppermute | solution.py:27
  209.3 10.5 %collective-permute-done.10 = bf16[512,512]{1,0:T(8,128)(2,1)S(1)} collective-permute-done((bf16[512,512]{1,0:T(8,128)(2,1)S(1)}, bf16[512,512]{1,0:T(8,128)(2,1)S(1)}, u32[]{:S(2)}, u32[]{:S(2)}) %collective-permute-start.10) | collective-permute-done | bytes 524320 | tf_op jit(solution)/shard_map/ppermute | solution.py:27
  221.0 5.8 %collective-permute-done.16.refs_5_ = bf16[2,512,512]{2,1,0:T(8,128)(2,1)} collective-permute-done((bf16[2,512,512]{2,1,0:T(8,128)(2,1)S(1)}, bf16[2,512,512]{2,1,0:T(8,128)(2,1)}, u32[]{:S(2)}, u32[]{:S(2)}) %collective-permute-start.16) | collective-permute-done | bytes 1048608 | tf_op jit(solution)/shard_map/ppermute | solution.py:32
  227.7 11.7 %muon.2 = (bf16[3,512,512]{2,1,0:T(8,128)(2,1)}, bf16[3,256,512]{2,1,0:T(8,128)(2,1)}, bf16[3,512,512]{2,1,0:T(8,128)(2,1)}) custom-call(s32[2]{0:T(128)} %pad_add_fusion.4.core_ref.scalar_ref, bf16[3,256,512]{2,1,0:T(8,128)(2,1)} %copy-done.9, bf16[3,256,512]{2,1,0:T(8,128)(2,1)} %copy-done.22, f32[3,2,512,512]{3,2,1,0:T(8,128)} %state_ref.1), custom_call_target="tpu_custom_call" | custom-call | flops 4831838208 | bytes 3145728 | tf_op jit(solution)/shard_map/muon/pallas_call | solution.py:202
  245.4 19.0 %attend.6 = (f32[4,2,512,256]{3,2,1,0:T(8,128)}, f32[4,2,512,128]{3,2,1,0:T(8,128)}) custom-call(s32[6]{0:T(128)} %pad_add_fusion.6.ids_ref, bf16[2,512,512]{2,1,0:T(8,128)(2,1)} %pad_maximum_fusion.5.query_ref, bf16[2,512,512]{2,1,0:T(8,128)(2,1)} %copy-done, bf16[2,512,512]{2,1,0:T(8,128)(2,1)} %copy-done.4, bf16[2,512,512]{2,1,0:T(8,128)(2,1)} %copy-done.18, ...), custom_call_target="tpu_custom_call" | custom-call | flops 5368709120 | bytes 4194304 | tf_op jit(solution)/shard_map/attend/pallas_call | solution.py:355
  265.4 27.6 %attend.7 = bf16[2,512,512]{2,1,0:T(8,128)(2,1)} custom-call(s32[10]{0:T(128)} %pad_add_fusion.5.ids_ref, bf16[2,512,512]{2,1,0:T(8,128)(2,1)} %pad_maximum_fusion.5.query_ref, bf16[2,512,512]{2,1,0:T(8,128)(2,1)} %collective-permute-done.2.refs_0_, bf16[2,512,512]{2,1,0:T(8,128)(2,1)} %copy-done.14, bf16[2,512,512]{2,1,0:T(8,128)(2,1)} %copy-done.15, ...), custom_call_target="tpu_custom_call" | custom-call | flops 5368709120 | bytes 8388608 | tf_op jit(solution)/shard_map/attend/pallas_call | solution.py:355
  297.4 11.9 %collective-permute-done.21 = bf16[512,512]{1,0:T(8,128)(2,1)S(1)} collective-permute-done((bf16[512,512]{1,0:T(8,128)(2,1)S(1)}, bf16[512,512]{1,0:T(8,128)(2,1)S(1)}, u32[]{:S(2)}, u32[]{:S(2)}) %collective-permute-start.21) | collective-permute-done | bytes 524320 | tf_op jit(solution)/shard_map/ppermute | solution.py:27
  309.4 10.0 %convolution_convert_fusion = bf16[512,4096]{1,0:T(8,128)(2,1)} fusion(bf16[1024,4096]{1,0:T(8,128)(2,1)} %param.13, bf16[512,512]{1,0:T(8,128)(2,1)S(1)} %get-tuple-element.59, bf16[512,512]{1,0:T(8,128)(2,1)S(1)} %get-tuple-element.58), kind=kOutput, calls=%fused_computation | convolution fusion | flops 4299161600 | bytes 13631488 | tf_op jit(solution)/shard_map/dot_general | solution.py:478
  320.2 5.7 %grads_first.3.sum_ref = f32[3,512,512]{2,1,0:T(8,128)} custom-call(bf16[2,512,512]{2,1,0:T(8,128)(2,1)} %copy-done, f32[512,128]{1,0:T(8,128)} %broadcast_in_dim.41.rate_ref, bf16[3,512,512]{2,1,0:T(8,128)(2,1)} %get-tuple-element.34.weight_ref), custom_call_target="tpu_custom_call" | custom-call | flops 1610612736 | bytes 4194304 | tf_op jit(solution)/shard_map/grads_first/pallas_call | solution.py:118
  326.7 6.9 %grads_second.3 = (bf16[3,256,512]{2,1,0:T(8,128)(2,1)}, bf16[3,256,512]{2,1,0:T(8,128)(2,1)}) custom-call(s32[1]{0:T(128)} %bitcast.25.core_ref, bf16[2,512,512]{2,1,0:T(8,128)(2,1)} %copy-done.4, f32[512,128]{1,0:T(8,128)} %broadcast_in_dim.39.rate_ref, bf16[3,512,512]{2,1,0:T(8,128)(2,1)} %get-tuple-element.34.weight_ref, f32[3,512,512]{2,1,0:T(8,128)} %grads_first.3.sum_ref), custom_call_target="tpu_custom_call" | custom-call | flops 1610612736 | bytes 7340032 | tf_op jit(solution)/shard_map/grads_second/pallas_call | solution.py:133
  340.4 18.1 %collective-permute-done.25 = bf16[3,256,512]{2,1,0:T(8,128)(2,1)S(1)} collective-permute-done((bf16[3,256,512]{2,1,0:T(8,128)(2,1)S(1)}, bf16[3,256,512]{2,1,0:T(8,128)(2,1)S(1)}, u32[]{:S(2)}, u32[]{:S(2)}) %collective-permute-start.25) | collective-permute-done | bytes 786464 | tf_op jit(solution)/shard_map/ppermute | solution.py:27
  361.9 9.6 %muon.3 = (bf16[3,512,512]{2,1,0:T(8,128)(2,1)}, bf16[3,256,512]{2,1,0:T(8,128)(2,1)}) custom-call(s32[2]{0:T(128)} %pad_add_fusion.7.core_ref, bf16[3,256,512]{2,1,0:T(8,128)(2,1)} %copy-done.11, bf16[3,256,512]{2,1,0:T(8,128)(2,1)} %copy-done.23), custom_call_target="tpu_custom_call" | custom-call | flops 4831838208 | bytes 3145728 | tf_op jit(solution)/shard_map/muon/pallas_call | solution.py:202
  373.0 6.8 %collective-permute-done.22.refs_1_ = bf16[3,256,512]{2,1,0:T(8,128)(2,1)S(1)} collective-permute-done((bf16[3,256,512]{2,1,0:T(8,128)(2,1)S(1)}, bf16[3,256,512]{2,1,0:T(8,128)(2,1)S(1)}, u32[]{:S(2)}, u32[]{:S(2)}) %collective-permute-start.22) | collective-permute-done | bytes 786464 | tf_op jit(solution)/shard_map/ppermute | solution.py:27
  379.8 16.4 %collective-permute-done.27.refs_4_ = bf16[3,256,512]{2,1,0:T(8,128)(2,1)S(1)} collective-permute-done((bf16[3,256,512]{2,1,0:T(8,128)(2,1)}, bf16[3,256,512]{2,1,0:T(8,128)(2,1)S(1)}, u32[]{:S(2)}, u32[]{:S(2)}) %collective-permute-start.27) | collective-permute-done | bytes 786464 | tf_op jit(solution)/shard_map/ppermute | solution.py:27
  399.4 11.7 %finish.1 = f32[3,2,512,512]{3,2,1,0:T(8,128)} custom-call(s32[2]{0:T(128)} %pad_add_fusion.4.core_ref.scalar_ref, f32[3,2,512,512]{3,2,1,0:T(8,128)} %state_ref.1, bf16[3,512,512]{2,1,0:T(8,128)(2,1)} %get-tuple-element.39.refs_0_, bf16[3,256,512]{2,1,0:T(8,128)(2,1)} %copy-done.5, bf16[3,256,512]{2,1,0:T(8,128)(2,1)} %copy-done.7, ...), custom_call_target="tpu_custom_call" | custom-call | flops 31457280 | bytes 18874368 | tf_op jit(solution)/shard_map/finish/pallas_call | solution.py:258
  (146 shorter events, 96.1 us)
Async XLA Ops:
  7.2 403.9 %reduce-scatter.3.cloned.1.call-start = ((), (), s32[]{:S(2)}) async-start(), calls=%async_computation.2 | async-start | bytes 5242880 | tf_op jit(solution)/shard_map/reduce_scatter | solution.py:479
  9.9 26.3 %collective-permute-start = (bf16[2,512,512]{2,1,0:T(8,128)(2,1)S(1)}, bf16[2,512,512]{2,1,0:T(8,128)(2,1)}, u32[]{:S(2)}, u32[]{:S(2)}) collective-permute-start(bf16[2,512,512]{2,1,0:T(8,128)(2,1)S(1)} %pad_maximum_fusion.1), channel_id=1, source_target_pairs={{0,2},{1,3},{2,0},{3,1},{4,6},{5,7},{6,4},{7,5},{8,10},{9,11},{10,... | collective-permute-start | bytes 3145736 | tf_op jit(solution)/shard_map/ppermute | solution.py:27
  14.0 24.9 %collective-permute-start.2 = (bf16[2,512,512]{2,1,0:T(8,128)(2,1)}, bf16[2,512,512]{2,1,0:T(8,128)(2,1)}, u32[]{:S(2)}, u32[]{:S(2)}) collective-permute-start(bf16[2,512,512]{2,1,0:T(8,128)(2,1)} %pad_maximum_fusion.3.refs_0_.kv_ref), channel_id=1, source_target_pairs={{0,4},{1,5},{2,6},{3,7},{4,0},{5,1},{6,2},{7,3},{8,12},{9,13},{10,... | collective-permute-start | bytes 3145736 | tf_op jit(solution)/shard_map/ppermute | solution.py:27
  15.5 54.9 %collective-permute-start.6 = (bf16[2,512,512]{2,1,0:T(8,128)(2,1)}, bf16[2,512,512]{2,1,0:T(8,128)(2,1)}, u32[]{:S(2)}, u32[]{:S(2)}) collective-permute-start(bf16[2,512,512]{2,1,0:T(8,128)(2,1)} %pad_maximum_fusion.3.refs_0_.kv_ref), channel_id=1, source_target_pairs={{0,1},{1,0},{2,3},{3,2},{4,5},{5,4},{6,7},{7,6},{8,9},{9,8},{10,11... | collective-permute-start | bytes 3145736 | tf_op jit(solution)/shard_map/ppermute | solution.py:27
  38.9 23.9 %collective-permute-start.3 = (bf16[2,512,512]{2,1,0:T(8,128)(2,1)}, bf16[2,512,512]{2,1,0:T(8,128)(2,1)S(1)}, u32[]{:S(2)}, u32[]{:S(2)}) collective-permute-start(bf16[2,512,512]{2,1,0:T(8,128)(2,1)} %collective-permute-done.refs_1_.kv_ref), channel_id=1, source_target_pairs={{0,4},{1,5},{2,6},{3,7},{4,0},{5,1},{6,2},{7,3},{8,12},{9,13},{10,... | collective-permute-start | bytes 3145736 | tf_op jit(solution)/shard_map/ppermute | solution.py:27
  46.5 23.9 %collective-permute-start.7 = (bf16[2,512,512]{2,1,0:T(8,128)(2,1)}, bf16[2,512,512]{2,1,0:T(8,128)(2,1)S(1)}, u32[]{:S(2)}, u32[]{:S(2)}) collective-permute-start(bf16[2,512,512]{2,1,0:T(8,128)(2,1)} %collective-permute-done.refs_1_.kv_ref), channel_id=1, source_target_pairs={{0,1},{1,0},{2,3},{3,2},{4,5},{5,4},{6,7},{7,6},{8,9},{9,8},{10,11... | collective-permute-start | bytes 3145736 | tf_op jit(solution)/shard_map/ppermute | solution.py:27
  46.6 17.6 %collective-permute-start.1 = (bf16[512,512]{1,0:T(8,128)(2,1)S(1)}, bf16[512,512]{1,0:T(8,128)(2,1)S(1)}, u32[]{:S(2)}, u32[]{:S(2)}) collective-permute-start(bf16[512,512]{1,0:T(8,128)(2,1)S(1)} %get-tuple-element.25), channel_id=1, source_target_pairs={{0,2},{1,3},{2,0},{3,1},{4,6},{5,7},{6,4},{7,5},{8,10},{9,11},{10,... | collective-permute-start | bytes 1572872 | tf_op jit(solution)/shard_map/ppermute | solution.py:27
  47.2 43.3 %collective-permute-start.4 = (bf16[2,512,512]{2,1,0:T(8,128)(2,1)}, bf16[2,512,512]{2,1,0:T(8,128)(2,1)S(1)}, u32[]{:S(2)}, u32[]{:S(2)}) collective-permute-start(bf16[2,512,512]{2,1,0:T(8,128)(2,1)} %collective-permute-done.2.refs_0_), channel_id=1, source_target_pairs={{0,1},{1,0},{2,3},{3,2},{4,5},{5,4},{6,7},{7,6},{8,9},{9,8},{10,11... | collective-permute-start | bytes 3145736 | tf_op jit(solution)/shard_map/ppermute | solution.py:27
  62.8 27.6 %collective-permute-start.5 = (bf16[2,512,512]{2,1,0:T(8,128)(2,1)S(1)}, bf16[2,512,512]{2,1,0:T(8,128)(2,1)S(1)}, u32[]{:S(2)}, u32[]{:S(2)}) collective-permute-start(bf16[2,512,512]{2,1,0:T(8,128)(2,1)S(1)} %collective-permute-done.3.refs_1_), channel_id=1, source_target_pairs={{0,1},{1,0},{2,3},{3,2},{4,5},{5,4},{6,7},{7,6},{8,9},{9,8},{10,11... | collective-permute-start | bytes 3145736 | tf_op jit(solution)/shard_map/ppermute | solution.py:27
  121.5 289.6 %reduce-scatter.5.cloned.1.call-start = ((), (), s32[]{:S(2)}) async-start(), calls=%async_computation.3 | async-start | bytes 5242880 | tf_op jit(solution)/shard_map/reduce_scatter | solution.py:479
  137.7 27.1 %collective-permute-start.12 = (bf16[3,256,512]{2,1,0:T(8,128)(2,1)}, bf16[3,256,512]{2,1,0:T(8,128)(2,1)S(1)}, u32[]{:S(2)}, u32[]{:S(2)}) collective-permute-start(bf16[3,256,512]{2,1,0:T(8,128)(2,1)} %get-tuple-element.32), channel_id=1, source_target_pairs={{0,1},{1,0},{2,3},{3,2},{4,5},{5,4},{6,7},{7,6},{8,9},{9,8},{10,11... | collective-permute-start | bytes 2359304 | tf_op jit(solution)/shard_map/ppermute | solution.py:27
  143.2 25.1 %collective-permute-start.9 = (bf16[2,512,512]{2,1,0:T(8,128)(2,1)S(1)}, bf16[2,512,512]{2,1,0:T(8,128)(2,1)S(1)}, u32[]{:S(2)}, u32[]{:S(2)}) collective-permute-start(bf16[2,512,512]{2,1,0:T(8,128)(2,1)S(1)} %pad_maximum_fusion.4), channel_id=1, source_target_pairs={{0,2},{1,3},{2,0},{3,1},{4,6},{5,7},{6,4},{7,5},{8,10},{9,11},{10,... | collective-permute-start | bytes 3145736 | tf_op jit(solution)/shard_map/ppermute | solution.py:27
  144.7 43.6 %collective-permute-start.15 = (bf16[2,512,512]{2,1,0:T(8,128)(2,1)S(1)}, bf16[2,512,512]{2,1,0:T(8,128)(2,1)S(1)}, u32[]{:S(2)}, u32[]{:S(2)}) collective-permute-start(bf16[2,512,512]{2,1,0:T(8,128)(2,1)S(1)} %pad_maximum_fusion.6.refs_0_.kv_ref), channel_id=1, source_target_pairs={{0,4},{1,5},{2,6},{3,7},{8,12},{9,13},{10,14},{11,15},{16,20},{17,... | collective-permute-start | bytes 3145736 | tf_op jit(solution)/shard_map/ppermute | solution.py:32
  165.0 40.0 %collective-permute-start.13 = (bf16[3,256,512]{2,1,0:T(8,128)(2,1)S(1)}, bf16[3,256,512]{2,1,0:T(8,128)(2,1)S(1)}, u32[]{:S(2)}, u32[]{:S(2)}) collective-permute-start(bf16[3,256,512]{2,1,0:T(8,128)(2,1)S(1)} %add_convert_fusion.5), channel_id=1, source_target_pairs={{0,4},{1,5},{2,6},{3,7},{4,0},{5,1},{6,2},{7,3},{8,12},{9,13},{10,... | collective-permute-start | bytes 2359304 | tf_op jit(solution)/shard_map/ppermute | solution.py:27
  188.2 38.5 %collective-permute-start.16 = (bf16[2,512,512]{2,1,0:T(8,128)(2,1)S(1)}, bf16[2,512,512]{2,1,0:T(8,128)(2,1)}, u32[]{:S(2)}, u32[]{:S(2)}) collective-permute-start(bf16[2,512,512]{2,1,0:T(8,128)(2,1)S(1)} %collective-permute-done.9.refs_1_.kv_ref), channel_id=1, source_target_pairs={{0,4},{1,5},{2,6},{3,7},{8,12},{9,13},{10,14},{11,15},{16,20},{17,... | collective-permute-start | bytes 3145736 | tf_op jit(solution)/shard_map/ppermute | solution.py:32
  205.3 21.5 %collective-permute-start.14 = (bf16[3,256,512]{2,1,0:T(8,128)(2,1)S(1)}, bf16[3,256,512]{2,1,0:T(8,128)(2,1)S(1)}, u32[]{:S(2)}, u32[]{:S(2)}) collective-permute-start(bf16[3,256,512]{2,1,0:T(8,128)(2,1)S(1)} %add_convert_fusion.4.mine_ref), channel_id=1, source_target_pairs={{0,1},{1,0},{2,3},{3,2},{4,5},{5,4},{6,7},{7,6},{8,9},{9,8},{10,11... | collective-permute-start | bytes 2359304 | tf_op jit(solution)/shard_map/ppermute | solution.py:27
  206.9 37.5 %collective-permute-start.19 = (bf16[2,512,512]{2,1,0:T(8,128)(2,1)S(1)}, bf16[2,512,512]{2,1,0:T(8,128)(2,1)S(1)}, u32[]{:S(2)}, u32[]{:S(2)}) collective-permute-start(bf16[2,512,512]{2,1,0:T(8,128)(2,1)S(1)} %pad_maximum_fusion.6.refs_0_.kv_ref), channel_id=1, source_target_pairs={{0,1},{1,0},{2,3},{3,2},{4,5},{5,4},{6,7},{7,6},{8,9},{9,8},{10,11... | collective-permute-start | bytes 3145736 | tf_op jit(solution)/shard_map/ppermute | solution.py:27
  207.2 37.2 %collective-permute-start.20 = (bf16[2,512,512]{2,1,0:T(8,128)(2,1)S(1)}, bf16[2,512,512]{2,1,0:T(8,128)(2,1)}, u32[]{:S(2)}, u32[]{:S(2)}) collective-permute-start(bf16[2,512,512]{2,1,0:T(8,128)(2,1)S(1)} %collective-permute-done.9.refs_1_.kv_ref), channel_id=1, source_target_pairs={{0,1},{1,0},{2,3},{3,2},{4,5},{5,4},{6,7},{7,6},{8,9},{9,8},{10,11... | collective-permute-start | bytes 3145736 | tf_op jit(solution)/shard_map/ppermute | solution.py:27
  219.9 44.6 %collective-permute-start.17 = (bf16[2,512,512]{2,1,0:T(8,128)(2,1)S(1)}, bf16[2,512,512]{2,1,0:T(8,128)(2,1)}, u32[]{:S(2)}, u32[]{:S(2)}) collective-permute-start(bf16[2,512,512]{2,1,0:T(8,128)(2,1)S(1)} %collective-permute-done.15.refs_4_), channel_id=1, source_target_pairs={{0,1},{1,0},{2,3},{3,2},{4,5},{5,4},{6,7},{7,6},{8,9},{9,8},{10,11... | collective-permute-start | bytes 3145736 | tf_op jit(solution)/shard_map/ppermute | solution.py:27
  226.8 37.7 %collective-permute-start.18 = (bf16[2,512,512]{2,1,0:T(8,128)(2,1)}, bf16[2,512,512]{2,1,0:T(8,128)(2,1)S(1)}, u32[]{:S(2)}, u32[]{:S(2)}) collective-permute-start(bf16[2,512,512]{2,1,0:T(8,128)(2,1)} %collective-permute-done.16.refs_5_), channel_id=1, source_target_pairs={{0,1},{1,0},{2,3},{3,2},{4,5},{5,4},{6,7},{7,6},{8,9},{9,8},{10,11... | collective-permute-start | bytes 3145736 | tf_op jit(solution)/shard_map/ppermute | solution.py:27
  338.0 20.5 %collective-permute-start.25 = (bf16[3,256,512]{2,1,0:T(8,128)(2,1)S(1)}, bf16[3,256,512]{2,1,0:T(8,128)(2,1)S(1)}, u32[]{:S(2)}, u32[]{:S(2)}) collective-permute-start(bf16[3,256,512]{2,1,0:T(8,128)(2,1)S(1)} %add_convert_fusion.3), channel_id=1, source_target_pairs={{0,4},{1,5},{2,6},{3,7},{4,0},{5,1},{6,2},{7,3},{8,12},{9,13},{10,... | collective-permute-start | bytes 2359304 | tf_op jit(solution)/shard_map/ppermute | solution.py:27
  359.4 20.3 %collective-permute-start.22 = (bf16[3,256,512]{2,1,0:T(8,128)(2,1)S(1)}, bf16[3,256,512]{2,1,0:T(8,128)(2,1)S(1)}, u32[]{:S(2)}, u32[]{:S(2)}) collective-permute-start(bf16[3,256,512]{2,1,0:T(8,128)(2,1)S(1)} %copy-done.21), channel_id=1, source_target_pairs={{0,2},{1,3},{2,0},{3,1},{4,6},{5,7},{6,4},{7,5},{8,10},{9,11},{10,... | collective-permute-start | bytes 2359304 | tf_op jit(solution)/shard_map/ppermute | solution.py:27
  371.5 24.6 %collective-permute-start.27 = (bf16[3,256,512]{2,1,0:T(8,128)(2,1)}, bf16[3,256,512]{2,1,0:T(8,128)(2,1)S(1)}, u32[]{:S(2)}, u32[]{:S(2)}) collective-permute-start(bf16[3,256,512]{2,1,0:T(8,128)(2,1)} %get-tuple-element.47), channel_id=1, source_target_pairs={{0,2},{1,3},{2,0},{3,1},{4,6},{5,7},{6,4},{7,5},{8,10},{9,11},{10,... | collective-permute-start | bytes 2359304 | tf_op jit(solution)/shard_map/ppermute | solution.py:27
  379.8 16.4 %collective-permute-start.23 = (bf16[3,256,512]{2,1,0:T(8,128)(2,1)S(1)}, bf16[3,256,512]{2,1,0:T(8,128)(2,1)S(1)}, u32[]{:S(2)}, u32[]{:S(2)}) collective-permute-start(bf16[3,256,512]{2,1,0:T(8,128)(2,1)S(1)} %collective-permute-done.22.refs_1_), channel_id=1, source_target_pairs={{0,1},{1,0},{2,3},{3,2},{4,5},{5,4},{6,7},{7,6},{8,9},{9,8},{10,11... | collective-permute-start | bytes 2359304 | tf_op jit(solution)/shard_map/ppermute | solution.py:27
  (31 other events, 346.7 us)
Sparse Core Ops, SparseCore 0:
  121.6 100.8 reduce-scatter.2
  319.5 79.7 reduce-scatter.4
